TPU v7x, 32 devices: a whole 2x2x4 slice. The times are simulated.
32 devices in a mesh: chain: 4 (over y, x), row: 8 (over z, core).
Axes of the slice: x: 2, y: 2, z: 4, core: 2. Of those that a mesh axis runs over, the one named last changes fastest.
Arguments:
- right_side: float32 [131072, 128], P('row'), may hold values from -6 to 6
- factor: bfloat16 [131072, 1, 2048], P('row', None, 'chain'), may hold values from -0.125 to 0.125
- tile_scales: float32 [256, 1, 4], P('row', None, 'chain'), may hold values from 0.5 to 2
- diag_inverse: float32 [1, 512, 2048], P(None, None, 'chain'), may hold values from -0.25 to 0.25
Outputs:
- updated: float32 [131072, 128], P('row')
All inputs are finite; a program needn't handle non-finite values.
Results may differ from a plain program's by a relative error of at most 0.0031.
Values may be sent and summed in bfloat16 or wider, within the bound.
A program may use at most 128 MiB of HBM per device.

v0:
```python
import jax
import jax.numpy as jnp
from jax import lax
from jax.sharding import PartitionSpec as P


def spread(value, axis, source):
    kept = jnp.where(lax.axis_index(axis) == source, value, 0).astype(value.dtype)
    return lax.psum(kept, axis)


def local(right_side, factor, tile_scales, diag_inverse):
    chain_index = lax.axis_index("chain")
    row_index = lax.axis_index("row")
    chain_count = lax.axis_size("chain")
    local_rows, rhs_count = right_side.shape
    rounds = factor.shape[1]
    block_size = factor.shape[2]
    tile_count = local_rows // block_size
    block_count = rounds * chain_count
    window = block_count * block_size
    row_ids = row_index * local_rows + jnp.arange(local_rows, dtype=jnp.int32)
    lead_chain = (chain_index == 0).astype(jnp.float32)
    zero = jnp.int32(0)

    def step(column, carry):
        carried, solved = carry
        round_index = column // chain_count
        owner_chain = column % chain_count
        block_start = column * block_size
        holder_row = block_start // local_rows
        offset = block_start % local_rows
        holder = row_index == holder_row
        own_rhs = lax.dynamic_slice(right_side, (offset, zero), (block_size, rhs_count))
        own_part = lax.dynamic_slice(carried, (offset, zero), (block_size, rhs_count))
        contrib = lead_chain * own_rhs - own_part
        inverse = lax.dynamic_index_in_dim(diag_inverse, round_index, 0, keepdims=False)
        residue = lax.psum(contrib, "chain")
        solved_now = jnp.dot(
            inverse, residue, precision=lax.Precision.HIGHEST, preferred_element_type=jnp.float32
        )
        solved_low = spread(solved_now.astype(jnp.bfloat16), "row", holder_row)

        def update(running):
            panel = lax.dynamic_index_in_dim(factor, round_index, 1, keepdims=False)
            product = jnp.dot(panel, solved_low, preferred_element_type=jnp.float32)
            tile_scale = lax.dynamic_index_in_dim(tile_scales, round_index, 1, keepdims=False)
            product = (
                product.reshape(tile_count, block_size, rhs_count) * tile_scale[:, :, None]
            ).reshape(local_rows, rhs_count)
            below = row_ids >= block_start + block_size
            return running + jnp.where(below[:, None], product, 0.0)

        def unchanged(running):
            return running

        carried = lax.cond(chain_index == owner_chain, update, unchanged, carried)
        store_mask = holder & (chain_index == owner_chain)
        previous = lax.dynamic_slice(solved, (offset, zero), (block_size, rhs_count))
        solved = lax.dynamic_update_slice(
            solved, jnp.where(store_mask, solved_now, previous), (offset, zero)
        )
        return (carried, solved)

    carried = jnp.zeros((local_rows, rhs_count), jnp.float32)
    solved = jnp.zeros((local_rows, rhs_count), jnp.float32)
    carried, solved = lax.fori_loop(0, block_count, step, (carried, solved))
    partial_out = jnp.where((row_ids < window)[:, None], solved, lead_chain * right_side - carried)
    return lax.psum(partial_out, "chain")


def solution(mesh):
    return jax.shard_map(
        local,
        mesh=mesh,
        in_specs=(
            P("row", None),
            P("row", None, "chain"),
            P("row", None, "chain"),
            P(None, None, "chain"),
        ),
        out_specs=P("row", None),
        check_vma=False,
    )
```

profile of v0, /device:TPU:11, one launch (start us, length us, event | category | flops | bytes accessed | tf_op | source)
XLA Modules:
  0.0 719.4 jit_solution(11307283123323036129)
XLA Ops:
  7.4 3.7 broadcast.16
  11.1 3.5 broadcast.16.clone.1
  14.6 482.2 %while.22 = (s32[]{:T(128)}, f32[16384,128]{1,0:T(8,128)}, f32[16384,128]{1,0:T(8,128)}, s32[]{:T(128)}, f32[]{:T(128)}, /*index=5*/f32[16384,128]{1,0:T(8,128)}...) while((s32[]{:T(128)}, f32[16384,128]{1,0:T(8,128)}, ...), condition=%wide.region_5.6_spmd.clone, body=%wide.region_0.5_spmd.clone.sunk | while | flops 2556919808 | bytes 58360652 | solution.py:67
  14.6 1.8 dynamic-slice_subtract_fusion.2
  16.5 1.0 constant_dynamic-slice_fusion.2
  17.7 44.6 %all-reduce.6.cloned.1.call-done = f32[512,128]{1,0:T(8,128)} async-done(((f32[512,128]{1,0:T(8,128)}), f32[512,128]{1,0:T(8,128)}) %all-reduce.6.cloned.1.call-update) | async-done | bytes 262160 | tf_op jit(solution)/shard_map/while/body/eval_jaxpr/psum | solution.py:38
  62.2 2.8 convert_select_fusion.2
  65.3 0.7 constant_dynamic-update-slice_fusion.2
  66.0 51.7 %all-reduce.8.cloned.1.call-done = bf16[512,128]{0,1:T(8,128)(2,1)} async-done(((bf16[512,128]{0,1:T(8,128)(2,1)}), bf16[512,128]{0,1:T(8,128)(2,1)}) %all-reduce.8.cloned.1.call-update) | async-done | bytes 131088 | tf_op jit(solution)/shard_map/while/body/eval_jaxpr/psum | solution.py:9
  117.8 1.8 dynamic-slice_subtract_fusion.2
  119.7 1.0 constant_dynamic-slice_fusion.2
  120.8 67.2 %all-reduce.6.cloned.1.call-done = f32[512,128]{1,0:T(8,128)} async-done(((f32[512,128]{1,0:T(8,128)}), f32[512,128]{1,0:T(8,128)}) %all-reduce.6.cloned.1.call-update) | async-done | bytes 262160 | tf_op jit(solution)/shard_map/while/body/eval_jaxpr/psum | solution.py:38
  188.0 2.9 convert_select_fusion.2
  191.8 51.7 %all-reduce.8.cloned.1.call-done = bf16[512,128]{0,1:T(8,128)(2,1)} async-done(((bf16[512,128]{0,1:T(8,128)(2,1)}), bf16[512,128]{0,1:T(8,128)(2,1)}) %all-reduce.8.cloned.1.call-update) | async-done | bytes 131088 | tf_op jit(solution)/shard_map/while/body/eval_jaxpr/psum | solution.py:9
  243.6 24.3 %conditional.3 = (f32[16384,128]{1,0:T(8,128)}) conditional(s32[]{:T(128)} %convert_element_type.40, f32[16384,128]{1,0:T(8,128)} %get-tuple-element.526, (s32[]{:T(128)}, s32[]{:T(128)}, bf16[16384,1,512]{2,0,1:T(8,128)(2,1)}, bf16[512,128]{0,1:T(8,128)(2,1)}, f32[32,1,1]{0,2,1:T(1,128)S(1)}, /*index=5*/f32[16384,128]{1,0:T(8,128)}, ...), branch_computations={%region_3.3_spmd, %region_4.4_spmd} | conditional | flops 2153807872 | bytes 50561180 | solution.py:57
  243.6 13.5 %broadcast_multiply_fusion = f32[32,512,128]{2,1,0:T(8,128)} fusion(f32[32]{0:T(128)S(1)} %bitcast.23, bf16[32,512,512]{2,1,0:T(8,128)(2,1)} %bitcast.22, bf16[512,128]{0,1:T(8,128)(2,1)} %get-tuple-element.392), kind=kOutput, calls=%fused_computation.3 | convolution fusion | flops 2149580800 | bytes 25297024 | tf_op jit(solution)/shard_map/while/body/eval_jaxpr/cond/branch_1_fun/dot_general | solution.py:46
  257.1 10.8 %fusion.2 = f32[16384,128]{1,0:T(8,128)} fusion(f32[16384,128]{1,0:T(8,128)} %get-tuple-element.342, f32[32,512,128]{2,1,0:T(8,128)} %broadcast_multiply_fusion, pred[16384]{0:T(1024)(128)(4,1)S(1)} %add_compare_fusion), kind=kLoop, calls=%fused_computation.2 | loop fusion | flops 4194304 | bytes 25182208 | tf_op jit(solution)/shard_map/while/body/eval_jaxpr/cond/branch_1_fun/add | solution.py:52
  267.9 1.8 dynamic-slice_subtract_fusion.2
  269.8 1.0 constant_dynamic-slice_fusion.2
  271.0 43.5 %all-reduce.6.cloned.1.call-done = f32[512,128]{1,0:T(8,128)} async-done(((f32[512,128]{1,0:T(8,128)}), f32[512,128]{1,0:T(8,128)}) %all-reduce.6.cloned.1.call-update) | async-done | bytes 262160 | tf_op jit(solution)/shard_map/while/body/eval_jaxpr/psum | solution.py:38
  314.5 2.9 convert_select_fusion.2
  317.5 0.7 constant_dynamic-update-slice_fusion.2
  318.2 51.8 %all-reduce.8.cloned.1.call-done = bf16[512,128]{0,1:T(8,128)(2,1)} async-done(((bf16[512,128]{0,1:T(8,128)(2,1)}), bf16[512,128]{0,1:T(8,128)(2,1)}) %all-reduce.8.cloned.1.call-update) | async-done | bytes 131088 | tf_op jit(solution)/shard_map/while/body/eval_jaxpr/psum | solution.py:9
  370.1 1.8 dynamic-slice_subtract_fusion.2
  372.0 1.0 constant_dynamic-slice_fusion.2
  373.1 68.1 %all-reduce.6.cloned.1.call-done = f32[512,128]{1,0:T(8,128)} async-done(((f32[512,128]{1,0:T(8,128)}), f32[512,128]{1,0:T(8,128)}) %all-reduce.6.cloned.1.call-update) | async-done | bytes 262160 | tf_op jit(solution)/shard_map/while/body/eval_jaxpr/psum | solution.py:38
  441.3 2.9 convert_select_fusion.2
  444.3 0.7 constant_dynamic-update-slice_fusion.2
  445.0 51.7 %all-reduce.8.cloned.1.call-done = bf16[512,128]{0,1:T(8,128)(2,1)} async-done(((bf16[512,128]{0,1:T(8,128)(2,1)}), bf16[512,128]{0,1:T(8,128)(2,1)}) %all-reduce.8.cloned.1.call-update) | async-done | bytes 131088 | tf_op jit(solution)/shard_map/while/body/eval_jaxpr/psum | solution.py:9
  496.8 11.9 %subtract_select_fusion = f32[16384,128]{1,0:T(8,128)} fusion(f32[16384,128]{1,0:T(8,128)} %get-tuple-element.362, f32[16384,128]{1,0:T(8,128)} %get-tuple-element.363, f32[16384,128]{1,0:T(8,128)} %get-tuple-element.577, f32[]{:T(128)} %convert_element_type.33, pred[16384]{0:T(1024)(128)(4,1)S(1)} %add_compare_fusion.1), kind=kLoop, calls=%fused_computation.13 | loop fusion | flops 6291456 | bytes 33570820 | tf_op jit(solution)/shard_map/jit(_where)/select_n | solution.py:68
  508.8 197.3 %all-reduce.4.cloned.1.call-done = f32[16384,128]{1,0:T(8,128)} async-done(((f32[16384,128]{1,0:T(8,128)}), f32[16384,128]{1,0:T(8,128)}) %all-reduce.4.cloned.1.call-update) | async-done | bytes 8388624 | tf_op jit(solution)/shard_map/psum | solution.py:69
  706.1 5.9 copy.32
  (44 shorter events, 2.5 us)
Async XLA Ops:
  7.4 7.2 copy-start
  7.4 7.2 copy-start.1
  14.6 47.6 %all-reduce.6.cloned.1.call-start = ((), (), s32[]{:S(2)}) async-start(), calls=%async_computation.1 | async-start | bytes 524288 | tf_op jit(solution)/shard_map/while/body/eval_jaxpr/psum | solution.py:38
  16.4 101.3 %all-reduce.8.cloned.1.call-start = ((), (), s32[]{:S(2)}) async-start(), calls=%async_computation.2 | async-start | bytes 262144 | tf_op jit(solution)/shard_map/while/body/eval_jaxpr/psum | solution.py:9
  117.8 70.3 %all-reduce.6.cloned.1.call-start = ((), (), s32[]{:S(2)}) async-start(), calls=%async_computation.1 | async-start | bytes 524288 | tf_op jit(solution)/shard_map/while/body/eval_jaxpr/psum | solution.py:38
  119.6 123.9 %all-reduce.8.cloned.1.call-start = ((), (), s32[]{:S(2)}) async-start(), calls=%async_computation.2 | async-start | bytes 262144 | tf_op jit(solution)/shard_map/while/body/eval_jaxpr/psum | solution.py:9
  267.9 46.6 %all-reduce.6.cloned.1.call-start = ((), (), s32[]{:S(2)}) async-start(), calls=%async_computation.1 | async-start | bytes 524288 | tf_op jit(solution)/shard_map/while/body/eval_jaxpr/psum | solution.py:38
  269.7 100.3 %all-reduce.8.cloned.1.call-start = ((), (), s32[]{:S(2)}) async-start(), calls=%async_computation.2 | async-start | bytes 262144 | tf_op jit(solution)/shard_map/while/body/eval_jaxpr/psum | solution.py:9
  370.0 71.2 %all-reduce.6.cloned.1.call-start = ((), (), s32[]{:S(2)}) async-start(), calls=%async_computation.1 | async-start | bytes 524288 | tf_op jit(solution)/shard_map/while/body/eval_jaxpr/psum | solution.py:38
  371.9 124.9 %all-reduce.8.cloned.1.call-start = ((), (), s32[]{:S(2)}) async-start(), calls=%async_computation.2 | async-start | bytes 262144 | tf_op jit(solution)/shard_map/while/body/eval_jaxpr/psum | solution.py:9
  496.8 209.3 %all-reduce.4.cloned.1.call-start = ((), (), s32[]{:S(2)}) async-start(), calls=%async_computation | async-start | bytes 16777216 | tf_op jit(solution)/shard_map/psum | solution.py:69
Sparse Core Ops, SparseCore 0:
  18.6 43.5 all-reduce.5
  65.4 52.3 all-reduce.7
  121.8 66.2 all-reduce.5
  191.2 52.3 all-reduce.7
  271.6 42.8 all-reduce.5
  317.6 52.3 all-reduce.7
  374.1 67.1 all-reduce.5
  444.4 52.2 all-reduce.7
Sparse Core Ops, SparseCore 1:
  508.9 197.1 all-reduce.3
where the time goes:
time: 721 us; the launch traced here: 719 us
  waiting for transfers between devices  628 us (87%)
  other arithmetic  30 us (4%)
  matrix products  24.9 us (3%)
  local copies, waits for them, and re-layouts  20.8 us (3%)
  between operations  14.8 us (2%)
    psum x4, waiting for transfers between devices, step(): residue = lax.psum(contrib, 'chain')  223 us
    psum x4, waiting for transfers between devices, spread(): return lax.psum(kept, axis)  207 us
    psum x1, waiting for transfers between devices, local(): return lax.psum(partial_out, 'chain')  197 us
  transfers between devices with their start and end apart: 9, of which 9 were waited for; matrix products, arithmetic and copies ran while one was open for 1% of the time, Pallas kernels for 0%

commit v1 on v0

v1 whole, which is shorter than its diff:
```python
import functools

import jax
import jax.numpy as jnp
from jax import lax
from jax.experimental import pallas as pl
from jax.experimental.pallas import tpu as pltpu
from jax.sharding import PartitionSpec as P

MESH = pl.DeviceIdType.MESH
SUB = 2


def kernel(chains, rows, rhs_ref, fac_ref, scale_ref, inv_ref, out_ref,
           fac, acc, inv, res, low, con_out, con_in, rel_out, dir_out, cmb_out, rel_in, dir_in, cmb_in, own,
           load_sem, xs_send, x_recv, cs_send, c_recv,
           rel_s, rel_r, dir_s, dir_r, cmb_s, cmb_r, ag_s, ag_r, fw_s, fw_r, own_sem):
    me = lax.axis_index("chain")
    row = lax.axis_index("row")
    local_rows, width = fac.shape
    tile = width
    window = chains * tile
    quarter = local_rows // 4
    half = quarter // 2
    piece = half // SUB
    peer = (me + 1 - 2 * (me % 2), me + 2 - 4 * (me // 2))
    across = 3 - me

    first = pltpu.make_async_copy(fac_ref.at[pl.ds(0, window)], fac.at[pl.ds(0, window)], load_sem.at[0])
    inv_load = pltpu.make_async_copy(inv_ref, inv, load_sem.at[1])
    own_load = pltpu.make_async_copy(rhs_ref.at[pl.ds(me * quarter, quarter)], acc, load_sem.at[2])
    res_load = pltpu.make_async_copy(rhs_ref.at[pl.ds(me * tile, tile)], res, load_sem.at[3])
    rest = None
    if local_rows > window:
        rest = pltpu.make_async_copy(
            fac_ref.at[pl.ds(window, local_rows - window)],
            fac.at[pl.ds(window, local_rows - window)], load_sem.at[4])

    @pl.when(row == 0)
    def _():
        inv_load.start()
        res_load.start()

    first.start()

    barrier = pltpu.get_barrier_semaphore()

    def greet(chain_to, row_to):
        pl.semaphore_signal(barrier, inc=1, device_id={"chain": chain_to, "row": row_to}, device_id_type=MESH)

    for hop in range(1, chains):
        greet(lax.rem(me + hop, chains), row)
    heads = [r for r in range(2, rows, 2)] + [1]

    @pl.when(row == 0)
    def _():
        for r in heads:
            greet(me, r)
        pl.semaphore_wait(barrier, chains - 1 + len(heads))

    @pl.when((row > 0) & (row % 2 == 0))
    def _():
        greet(me, 0)
        greet(me, row + 1)
        pl.semaphore_wait(barrier, chains - 1 + 2)

    @pl.when(row % 2 == 1)
    def _():
        greet(me, row - 1)
        pl.semaphore_wait(barrier, chains - 1 + 1)

    if rest is not None:
        rest.start()
    own_load.start()

    def send_low(row_to, sem):
        return pltpu.make_async_remote_copy(
            src_ref=low, dst_ref=low, send_sem=xs_send.at[sem], recv_sem=x_recv,
            device_id={"chain": me, "row": row_to}, device_id_type=MESH)

    def send_con(chain_to):
        return pltpu.make_async_remote_copy(
            src_ref=con_out.at[chain_to], dst_ref=con_in.at[me], send_sem=cs_send.at[chain_to],
            recv_sem=c_recv.at[me], device_id={"chain": chain_to, "row": row}, device_id_type=MESH)

    def recv_con(source):
        return pltpu.make_async_remote_copy(
            src_ref=con_out.at[source], dst_ref=con_in.at[source], send_sem=cs_send.at[source],
            recv_sem=c_recv.at[source], device_id={"chain": source, "row": row}, device_id_type=MESH)

    first.wait()

    @pl.when(row == 0)
    def _():
        inv_load.wait()
        res_load.wait()
        for j in range(chains - 1):
            @pl.when(j < me)
            def _():
                recv_con(j).wait_recv()
                res[...] = res[...] - con_in[j]
        solved = jnp.dot(inv[...], res[...], precision=lax.Precision.HIGHEST,
                         preferred_element_type=jnp.float32)
        low[...] = solved.astype(jnp.bfloat16)
        for i in range(1, chains):
            @pl.when(i > me)
            def _():
                con_out[i] = scale_ref[i] * jnp.dot(
                    fac[pl.ds(i * tile, tile), :], low[...], preferred_element_type=jnp.float32)
                send_con(i).start()
        for at, r in enumerate(heads):
            send_low(r, at).start()

    @pl.when(row > 0)
    def _():
        send_low(0, 0).wait_recv()

    @pl.when((row > 0) & (row % 2 == 0))
    def _():
        send_low(row + 1, 0).start()

    if rest is not None:
        rest.wait()
    own_load.wait()

    step = min(piece, tile)

    def partial(start, put):
        def body(t, carry):
            at = pl.multiple_of(start + t * step, step)
            index = at // tile
            value = scale_ref[index] * jnp.dot(fac[pl.ds(at, step), :], low[...], preferred_element_type=jnp.float32)
            put(t * step, value)

            @pl.when((row == 0) & (at < window))
            def _():
                keep = jnp.where(index == me, -1.0, 0.0)
                put(t * step, keep * low[pl.ds(at - index * tile, step), :].astype(jnp.float32))
            return carry
        lax.fori_loop(0, piece // step, body, 0)

    def putter(ref, a, s):
        def put(offset, value):
            ref[a, s, pl.ds(offset, step), :] = value.astype(jnp.bfloat16)
        return put

    def message(src, dst, send, recv, a, s):
        return pltpu.make_async_remote_copy(
            src_ref=src.at[a, s], dst_ref=dst.at[a, s], send_sem=send.at[a, s], recv_sem=recv.at[a, s],
            device_id={"chain": peer[a], "row": row}, device_id_type=MESH)

    def rel(a, s):
        return message(rel_out, rel_in, rel_s, rel_r, a, s)

    def direct(a, s):
        return message(dir_out, dir_in, dir_s, dir_r, a, s)

    def combined(a, s):
        return message(cmb_out, cmb_in, cmb_s, cmb_r, a, s)

    for s in range(SUB):
        for a in range(2):
            partial(across * quarter + (1 - a) * half + s * piece, putter(rel_out, a, s))
            rel(a, s).start()
    for s in range(SUB):
        for a in range(2):
            partial(peer[a] * quarter + (1 - a) * half + s * piece, putter(dir_out, a, s))
            direct(a, s).start()
    for s in range(SUB):
        for a in range(2):
            partial(peer[a] * quarter + a * half + s * piece, putter(cmb_out, a, s))

    @pl.when((row == 0) & (me * quarter < window))
    def _():
        masked = min(quarter, window)

        def wipe(t, carry):
            at = pl.multiple_of(t * step, step)

            @pl.when(me * quarter + at < window)
            def _():
                acc[pl.ds(at, step), :] = jnp.zeros((step, acc.shape[1]), jnp.float32)
            return carry
        lax.fori_loop(0, masked // step, wipe, 0)

    for h in range(2):
        for s in range(SUB):
            base = h * half + s * piece

            def body(t, carry, base=base):
                spot = pl.multiple_of(base + t * step, step)
                at = pl.multiple_of(me * quarter + spot, step)
                index = at // tile
                inside = (row == 0) & (at < window)

                @pl.when(jnp.logical_not(inside))
                def _():
                    acc[pl.ds(spot, step), :] -= scale_ref[index] * jnp.dot(
                        fac[pl.ds(at, step), :], low[...], preferred_element_type=jnp.float32)

                @pl.when(inside & (index == me))
                def _():
                    acc[pl.ds(spot, step), :] = low[pl.ds(at - index * tile, step), :].astype(jnp.float32)
                return carry
            lax.fori_loop(0, piece // step, body, 0)

    def where_is(block, h, s):
        return pl.ds(pl.multiple_of(block * quarter + h * half + s * piece, piece), piece)

    def spread(a, h, s):
        return pltpu.make_async_remote_copy(
            src_ref=own.at[h, s], dst_ref=out_ref.at[where_is(me, h, s)],
            send_sem=ag_s.at[a, h, s], recv_sem=ag_r.at[a, h, s],
            device_id={"chain": peer[a], "row": row}, device_id_type=MESH)

    def arrived(a, h, s):
        return pltpu.make_async_remote_copy(
            src_ref=own.at[h, s], dst_ref=out_ref.at[where_is(peer[a], h, s)],
            send_sem=ag_s.at[a, h, s], recv_sem=ag_r.at[a, h, s],
            device_id={"chain": peer[a], "row": row}, device_id_type=MESH)

    def forward(a, s):
        spot = out_ref.at[where_is(peer[a], a, s)]
        return pltpu.make_async_remote_copy(
            src_ref=spot, dst_ref=spot, send_sem=fw_s.at[a, s], recv_sem=fw_r.at[a, s],
            device_id={"chain": peer[1 - a], "row": row}, device_id_type=MESH)

    def forwarded(a, s):
        spot = out_ref.at[where_is(across, a, s)]
        return pltpu.make_async_remote_copy(
            src_ref=spot, dst_ref=spot, send_sem=fw_s.at[a, s], recv_sem=fw_r.at[a, s],
            device_id={"chain": peer[1 - a], "row": row}, device_id_type=MESH)

    def keep(h, s):
        return pltpu.make_async_copy(own.at[h, s], out_ref.at[where_is(me, h, s)], own_sem.at[h, s])

    for s in range(SUB):
        for a in range(2):
            rel(1 - a, s).wait_recv()
            cmb_out[a, s] = (cmb_out[a, s].astype(jnp.float32) + rel_in[1 - a, s].astype(jnp.float32)).astype(jnp.bfloat16)
            combined(a, s).start()
    for s in range(SUB):
        for h in range(2):
            direct(1 - h, s).wait_recv()
            combined(h, s).wait_recv()
            own[h, s] = (acc[pl.ds(h * half + s * piece, piece), :] - dir_in[1 - h, s].astype(jnp.float32)
                         - cmb_in[h, s].astype(jnp.float32)).astype(jnp.bfloat16)
            spread(h, h, s).start()
            spread(1 - h, h, s).start()
            keep(h, s).start()
    for s in range(SUB):
        for a in range(2):
            arrived(a, a, s).wait_recv()
            forward(a, s).start()
    for s in range(SUB):
        for a in range(2):
            arrived(a, 1 - a, s).wait_recv()
            forwarded(a, s).wait_recv()
            rel(a, s).wait_send()
            direct(a, s).wait_send()
            combined(a, s).wait_send()
            spread(a, 0, s).wait_send()
            spread(a, 1, s).wait_send()
            forward(a, s).wait_send()
            keep(a, s).wait()

    @pl.when(row == 0)
    def _():
        for i in range(1, chains):
            @pl.when(i > me)
            def _():
                send_con(i).wait_send()
        for at, r in enumerate(heads):
            send_low(r, at).wait_send()

    @pl.when((row > 0) & (row % 2 == 0))
    def _():
        send_low(row + 1, 0).wait_send()


def local(chains, rows, right_side, factor, tile_scales, diag_inverse):
    local_rows, rhs_count = right_side.shape
    width = factor.shape[2]
    factor = factor.reshape(local_rows, width)
    scales = tile_scales.reshape(-1)
    inverse = diag_inverse.reshape(width, width)
    half = local_rows // 8
    piece = half // SUB
    low = jnp.bfloat16
    pieces = pltpu.VMEM((2, SUB, piece, rhs_count), low)
    sems = pltpu.SemaphoreType.DMA((2, SUB))
    anywhere = pl.BlockSpec(memory_space=pl.ANY)
    heads = len(range(2, rows, 2)) + 1
    gathered = pl.pallas_call(
        functools.partial(kernel, chains, rows),
        out_shape=jax.ShapeDtypeStruct((local_rows, rhs_count), low),
        in_specs=[anywhere, anywhere, pl.BlockSpec(memory_space=pltpu.SMEM), anywhere],
        out_specs=anywhere,
        scratch_shapes=[
            pltpu.VMEM((local_rows, width), low),
            pltpu.VMEM((local_rows // 4, rhs_count), jnp.float32),
            pltpu.VMEM((width, width), jnp.float32),
            pltpu.VMEM((width, rhs_count), jnp.float32),
            pltpu.VMEM((width, rhs_count), low),
            pltpu.VMEM((chains, width, rhs_count), jnp.float32),
            pltpu.VMEM((chains, width, rhs_count), jnp.float32),
            pieces, pieces, pieces, pieces, pieces, pieces, pieces,
            pltpu.SemaphoreType.DMA((5,)),
            pltpu.SemaphoreType.DMA((heads,)),
            pltpu.SemaphoreType.DMA,
            pltpu.SemaphoreType.DMA((chains,)),
            pltpu.SemaphoreType.DMA((chains,)),
            sems, sems, sems, sems, sems, sems,
            pltpu.SemaphoreType.DMA((2, 2, SUB)),
            pltpu.SemaphoreType.DMA((2, 2, SUB)),
            sems, sems,
            sems,
        ],
        compiler_params=pltpu.CompilerParams(
            collective_id=0, has_side_effects=True, vmem_limit_bytes=48 * 2**20),
        cost_estimate=pl.CostEstimate(
            flops=2 * local_rows * width * rhs_count, bytes_accessed=2 * local_rows * width, transcendentals=0),
    )(right_side, factor, scales, inverse)
    return gathered.astype(jnp.float32)


def solution(mesh):
    return jax.shard_map(
        functools.partial(local, mesh.shape["chain"], mesh.shape["row"]),
        mesh=mesh,
        in_specs=(
            P("row", None),
            P("row", None, "chain"),
            P("row", None, "chain"),
            P(None, None, "chain"),
        ),
        out_specs=P("row", None),
        check_vma=False,
    )
```

time: 721 us -> 112 us (0.16)
  the two profiles are of different devices: /device:TPU:11 before, /device:TPU:27 now
where the time goes in v1:
time: 112 us; the launch traced here: 111 us
  Pallas kernels  106 us (95%)
  other arithmetic  3.69 us (3%)
  local copies, waits for them, and re-layouts  1.88 us (2%)
    pallas_call x1, Pallas kernels, local(): pl.pallas_call(functools.partial(kernel, chains, rows), out_shape=jax.Sha...  106 us
    convert_element_type x1, other arithmetic, local(): return gathered.astype(jnp.float32)  3.69 us

profile of v1, /device:TPU:27, one launch (start us, length us, event | category | flops | bytes accessed | tf_op | source)
XLA Modules:
  0.0 111.4 jit_solution(14640498482292569122)
XLA Ops:
  0.0 0.0 copy-start
  0.0 1.2 %copy-done = f32[1,512,512]{2,1,0:T(8,128)S(1)} copy-done((f32[1,512,512]{2,1,0:T(8,128)S(1)}, f32[1,512,512]{2,1,0:T(8,128)}, u32[]{:S(2)}) %copy-start) | copy-done | bytes 1048600
  1.2 0.0 copy-start.1
  1.2 0.7 copy-done.1
  1.9 105.8 %shard_map.46 = bf16[16384,128]{1,0:T(8,128)(2,1)S(1)} custom-call(f32[16384,128]{1,0:T(8,128)} %rhs_ref.1, bf16[16384,512]{1,0:T(8,128)(2,1)} %bitcast.5, f32[32]{0:T(128)S(1)} %bitcast.4, f32[512,512]{1,0:T(8,128)S(1)} %bitcast.3), custom_call_target="tpu_custom_call" | custom-call | flops 2147483648 | bytes 16777216 | tf_op jit(solution)/shard_map/pallas_call | solution.py:294
  107.7 3.7 %convert_element_type.3 = f32[16384,128]{1,0:T(8,128)} convert(bf16[16384,128]{1,0:T(8,128)(2,1)S(1)} %shard_map.46) | non-fusion elementwise | flops 2097152 | bytes 12582912 | tf_op jit(solution)/shard_map/convert_element_type | solution.py:324
Async XLA Ops:
  0.0 1.2 %copy-start = (f32[1,512,512]{2,1,0:T(8,128)S(1)}, f32[1,512,512]{2,1,0:T(8,128)}, u32[]{:S(2)}) copy-start(f32[1,512,512]{2,1,0:T(8,128)} %param.7) | copy-start | bytes 3145732
  1.2 0.7 copy-start.1

commit v2 on v1

--- a/solution.py
+++ b/solution.py
@@ -8,11 +8,11 @@
 from jax.sharding import PartitionSpec as P
 
 MESH = pl.DeviceIdType.MESH
-SUB = 2
+SUB = 4
 
 
 def kernel(chains, rows, rhs_ref, fac_ref, scale_ref, inv_ref, out_ref,
-           fac, acc, inv, res, low, con_out, con_in, rel_out, dir_out, cmb_out, rel_in, dir_in, cmb_in, own,
+           fac, acc, inv, inv_high, inv_low, res, low, con_out, con_in, rel_out, dir_out, cmb_out, rel_in, dir_in, cmb_in, own,
            load_sem, xs_send, x_recv, cs_send, c_recv,
            rel_s, rel_r, dir_s, dir_r, cmb_s, cmb_r, ag_s, ag_r, fw_s, fw_r, own_sem):
     me = lax.axis_index("chain")
@@ -50,7 +50,7 @@
 
     for hop in range(1, chains):
         greet(lax.rem(me + hop, chains), row)
-    heads = [r for r in range(2, rows, 2)] + [1]
+    heads = [r for r in range(2, rows, 2)][::-1] + [1]
 
     @pl.when(row == 0)
     def _():
@@ -93,14 +93,21 @@
     @pl.when(row == 0)
     def _():
         inv_load.wait()
+        inv_high[...] = inv[...].astype(jnp.bfloat16)
+        inv_low[...] = (inv[...] - inv_high[...].astype(jnp.float32)).astype(jnp.bfloat16)
         res_load.wait()
         for j in range(chains - 1):
             @pl.when(j < me)
             def _():
                 recv_con(j).wait_recv()
                 res[...] = res[...] - con_in[j]
-        solved = jnp.dot(inv[...], res[...], precision=lax.Precision.HIGHEST,
-                         preferred_element_type=jnp.float32)
+        high = res[...].astype(jnp.bfloat16)
+        rest_part = (res[...] - high.astype(jnp.float32)).astype(jnp.bfloat16)
+        wide = jnp.dot(inv_high[...], jnp.concatenate([high, rest_part], axis=1),
+                       preferred_element_type=jnp.float32)
+        count = high.shape[1]
+        solved = wide[:, :count] + (wide[:, count:] + jnp.dot(
+            inv_low[...], high, preferred_element_type=jnp.float32))
         low[...] = solved.astype(jnp.bfloat16)
         for i in range(1, chains):
             @pl.when(i > me)
@@ -219,17 +226,23 @@
             send_sem=ag_s.at[a, h, s], recv_sem=ag_r.at[a, h, s],
             device_id={"chain": peer[a], "row": row}, device_id_type=MESH)
 
-    def forward(a, s):
-        spot = out_ref.at[where_is(peer[a], a, s)]
-        return pltpu.make_async_remote_copy(
-            src_ref=spot, dst_ref=spot, send_sem=fw_s.at[a, s], recv_sem=fw_r.at[a, s],
+    def forward(a, h, s):
+        spot = out_ref.at[where_is(peer[a], h, s)]
+        return pltpu.make_async_remote_copy(
+            src_ref=spot, dst_ref=spot, send_sem=fw_s.at[a, h, s], recv_sem=fw_r.at[a, h, s],
             device_id={"chain": peer[1 - a], "row": row}, device_id_type=MESH)
 
-    def forwarded(a, s):
-        spot = out_ref.at[where_is(across, a, s)]
-        return pltpu.make_async_remote_copy(
-            src_ref=spot, dst_ref=spot, send_sem=fw_s.at[a, s], recv_sem=fw_r.at[a, s],
+    def forwarded(a, h, s):
+        spot = out_ref.at[where_is(across, h, s)]
+        return pltpu.make_async_remote_copy(
+            src_ref=spot, dst_ref=spot, send_sem=fw_s.at[a, h, s], recv_sem=fw_r.at[a, h, s],
             device_id={"chain": peer[1 - a], "row": row}, device_id_type=MESH)
+
+    def forwards(a, h):
+        return me < 3 if h == a else me == 0
+
+    def is_forwarded(a, h):
+        return me != 1 + a if h == a else me == 2 - a
 
     def keep(h, s):
         return pltpu.make_async_copy(own.at[h, s], out_ref.at[where_is(me, h, s)], own_sem.at[h, s])
@@ -248,20 +261,28 @@
             spread(h, h, s).start()
             spread(1 - h, h, s).start()
             keep(h, s).start()
-    for s in range(SUB):
-        for a in range(2):
-            arrived(a, a, s).wait_recv()
-            forward(a, s).start()
-    for s in range(SUB):
-        for a in range(2):
-            arrived(a, 1 - a, s).wait_recv()
-            forwarded(a, s).wait_recv()
+    halves = [(a, h) for h in range(2) for a in range(2)]
+    for s in range(SUB):
+        for a, h in halves:
+            arrived(a, h, s).wait_recv()
+
+            @pl.when(forwards(a, h))
+            def _():
+                forward(a, h, s).start()
+    for s in range(SUB):
+        for a, h in halves:
+            @pl.when(is_forwarded(a, h))
+            def _():
+                forwarded(a, h, s).wait_recv()
+
+            @pl.when(forwards(a, h))
+            def _():
+                forward(a, h, s).wait_send()
+            spread(a, h, s).wait_send()
+        for a in range(2):
             rel(a, s).wait_send()
             direct(a, s).wait_send()
             combined(a, s).wait_send()
-            spread(a, 0, s).wait_send()
-            spread(a, 1, s).wait_send()
-            forward(a, s).wait_send()
             keep(a, s).wait()
 
     @pl.when(row == 0)
@@ -300,6 +321,8 @@
             pltpu.VMEM((local_rows, width), low),
             pltpu.VMEM((local_rows // 4, rhs_count), jnp.float32),
             pltpu.VMEM((width, width), jnp.float32),
+            pltpu.VMEM((width, width), low),
+            pltpu.VMEM((width, width), low),
             pltpu.VMEM((width, rhs_count), jnp.float32),
             pltpu.VMEM((width, rhs_count), low),
             pltpu.VMEM((chains, width, rhs_count), jnp.float32),
@@ -313,7 +336,8 @@
             sems, sems, sems, sems, sems, sems,
             pltpu.SemaphoreType.DMA((2, 2, SUB)),
             pltpu.SemaphoreType.DMA((2, 2, SUB)),
-            sems, sems,
+            pltpu.SemaphoreType.DMA((2, 2, SUB)),
+            pltpu.SemaphoreType.DMA((2, 2, SUB)),
             sems,
         ],
         compiler_params=pltpu.CompilerParams(

time: 112 us -> 105 us (0.938)
  the two profiles are of different devices: /device:TPU:27 before, /device:TPU:11 now
where the time goes in v2:
time: 105 us
  Pallas kernels  99 us (94%)
  other arithmetic  3.69 us (4%)
  local copies, waits for them, and re-layouts  1.88 us (2%)
    pallas_call x1, Pallas kernels, local(): pl.pallas_call(functools.partial(kernel, chains, rows), out_shape=jax.Sha...  99 us
    convert_element_type x1, other arithmetic, local(): return gathered.astype(jnp.float32)  3.69 us

profile of v2, /device:TPU:11, one launch (start us, length us, event | category | flops | bytes accessed | tf_op | source)
XLA Modules:
  0.0 104.6 jit_solution(6352049045184355819)
XLA Ops:
  0.0 0.0 copy-start
  0.0 1.2 %copy-done = f32[1,512,512]{2,1,0:T(8,128)S(1)} copy-done((f32[1,512,512]{2,1,0:T(8,128)S(1)}, f32[1,512,512]{2,1,0:T(8,128)}, u32[]{:S(2)}) %copy-start) | copy-done | bytes 1048600
  1.2 0.0 copy-start.1
  1.2 0.7 copy-done.1
  1.9 99.0 %shard_map.46 = bf16[16384,128]{1,0:T(8,128)(2,1)S(1)} custom-call(f32[16384,128]{1,0:T(8,128)} %rhs_ref.1, bf16[16384,512]{1,0:T(8,128)(2,1)} %bitcast.5, f32[32]{0:T(128)S(1)} %bitcast.4, f32[512,512]{1,0:T(8,128)S(1)} %bitcast.3), custom_call_target="tpu_custom_call" | custom-call | flops 2147483648 | bytes 16777216 | tf_op jit(solution)/shard_map/pallas_call | solution.py:315
  100.9 3.7 %convert_element_type.3 = f32[16384,128]{1,0:T(8,128)} convert(bf16[16384,128]{1,0:T(8,128)(2,1)S(1)} %shard_map.46) | non-fusion elementwise | flops 2097152 | bytes 12582912 | tf_op jit(solution)/shard_map/convert_element_type | solution.py:348
Async XLA Ops:
  0.0 1.2 %copy-start = (f32[1,512,512]{2,1,0:T(8,128)S(1)}, f32[1,512,512]{2,1,0:T(8,128)}, u32[]{:S(2)}) copy-start(f32[1,512,512]{2,1,0:T(8,128)} %param.7) | copy-start | bytes 3145732
  1.2 0.7 copy-start.1

commit v3 on v2

--- a/solution.py
+++ b/solution.py
@@ -8,6 +8,7 @@
 from jax.sharding import PartitionSpec as P
 
 MESH = pl.DeviceIdType.MESH
+FLIGHT = 4
 SUB = 4
 
 
@@ -156,6 +157,17 @@
             src_ref=src.at[a, s], dst_ref=dst.at[a, s], send_sem=send.at[a, s], recv_sem=recv.at[a, s],
             device_id={"chain": peer[a], "row": row}, device_id_type=MESH)
 
+    def received(dst, recv, a, s):
+        return pltpu.make_async_remote_copy(
+            src_ref=dst.at[a, s], dst_ref=dst.at[a, s], send_sem=recv.at[a, s], recv_sem=recv.at[a, s],
+            device_id={"chain": across, "row": row}, device_id_type=MESH)
+
+    def direct_from(a, s):
+        return received(dir_in, dir_r, a, s)
+
+    def combined_from(a, s):
+        return received(cmb_in, cmb_r, a, s)
+
     def rel(a, s):
         return message(rel_out, rel_in, rel_s, rel_r, a, s)
 
@@ -164,15 +176,23 @@
 
     def combined(a, s):
         return message(cmb_out, cmb_in, cmb_s, cmb_r, a, s)
+
+    flying = ([], [])
+
+    def issue(a, copy):
+        if len(flying[a]) >= FLIGHT:
+            flying[a][-FLIGHT].wait_send()
+        copy.start()
+        flying[a].append(copy)
 
     for s in range(SUB):
         for a in range(2):
             partial(across * quarter + (1 - a) * half + s * piece, putter(rel_out, a, s))
-            rel(a, s).start()
+            issue(a, rel(a, s))
     for s in range(SUB):
         for a in range(2):
             partial(peer[a] * quarter + (1 - a) * half + s * piece, putter(dir_out, a, s))
-            direct(a, s).start()
+            issue(a, direct(a, s))
     for s in range(SUB):
         for a in range(2):
             partial(peer[a] * quarter + a * half + s * piece, putter(cmb_out, a, s))
@@ -251,39 +271,38 @@
         for a in range(2):
             rel(1 - a, s).wait_recv()
             cmb_out[a, s] = (cmb_out[a, s].astype(jnp.float32) + rel_in[1 - a, s].astype(jnp.float32)).astype(jnp.bfloat16)
-            combined(a, s).start()
-    for s in range(SUB):
-        for h in range(2):
-            direct(1 - h, s).wait_recv()
-            combined(h, s).wait_recv()
-            own[h, s] = (acc[pl.ds(h * half + s * piece, piece), :] - dir_in[1 - h, s].astype(jnp.float32)
-                         - cmb_in[h, s].astype(jnp.float32)).astype(jnp.bfloat16)
-            spread(h, h, s).start()
-            spread(1 - h, h, s).start()
+            issue(a, combined(a, s))
+    flip = jnp.where(me == 2, 1, 0)
+    for k in range(2):
+        h = k + (1 - 2 * k) * flip
+        for s in range(SUB):
+            direct_from(1 - h, s).wait_recv()
+            combined_from(h, s).wait_recv()
+            own[h, s] = (acc[pl.ds(pl.multiple_of(h * half + s * piece, piece), piece), :]
+                         - dir_in[1 - h, s].astype(jnp.float32) - cmb_in[h, s].astype(jnp.float32)).astype(jnp.bfloat16)
+            for a in range(2):
+                issue(a, spread(a, h, s))
             keep(h, s).start()
-    halves = [(a, h) for h in range(2) for a in range(2)]
-    for s in range(SUB):
-        for a, h in halves:
-            arrived(a, h, s).wait_recv()
-
-            @pl.when(forwards(a, h))
-            def _():
-                forward(a, h, s).start()
-    for s in range(SUB):
-        for a, h in halves:
-            @pl.when(is_forwarded(a, h))
-            def _():
-                forwarded(a, h, s).wait_recv()
-
-            @pl.when(forwards(a, h))
-            def _():
-                forward(a, h, s).wait_send()
-            spread(a, h, s).wait_send()
-        for a in range(2):
-            rel(a, s).wait_send()
-            direct(a, s).wait_send()
-            combined(a, s).wait_send()
-            keep(a, s).wait()
+    turns = [(a, (k + a) % 2, s) for k in range(2) for s in range(SUB) for a in range(2)]
+    for a, h, s in turns:
+        arrived(a, h, s).wait_recv()
+
+        @pl.when(forwards(a, h))
+        def _():
+            forward(a, h, s).start()
+    for a, h, s in turns:
+        @pl.when(is_forwarded(a, h))
+        def _():
+            forwarded(a, h, s).wait_recv()
+
+        @pl.when(forwards(a, h))
+        def _():
+            forward(a, h, s).wait_send()
+        if a == 0:
+            keep(h, s).wait()
+    for a in range(2):
+        for copy in flying[a][-FLIGHT:]:
+            copy.wait_send()
 
     @pl.when(row == 0)
     def _():

time: 105 us -> 105 us (level); the launches traced: 105 us -> 103 us
  Pallas kernels: 99 us -> 97 us
    pallas_call x1, Pallas kernels: 99 us -> 97 us  [local(): pl.pallas_call(functools.partial(kernel, chains, rows), out_shape=jax.Sha...]
where the time goes in v3:
time: 105 us; the launch traced here: 103 us
  Pallas kernels  97 us (92%)
  other arithmetic  3.69 us (4%)
  local copies, waits for them, and re-layouts  1.88 us (2%)
    pallas_call x1, Pallas kernels, local(): pl.pallas_call(functools.partial(kernel, chains, rows), out_shape=jax.Sha...  97 us
    convert_element_type x1, other arithmetic, local(): return gathered.astype(jnp.float32)  3.69 us

profile of v3, /device:TPU:11, one launch (start us, length us, event | category | flops | bytes accessed | tf_op | source)
XLA Modules:
  0.0 102.6 jit_solution(3163007685283348332)
XLA Ops:
  0.0 0.0 copy-start
  0.0 1.2 %copy-done = f32[1,512,512]{2,1,0:T(8,128)S(1)} copy-done((f32[1,512,512]{2,1,0:T(8,128)S(1)}, f32[1,512,512]{2,1,0:T(8,128)}, u32[]{:S(2)}) %copy-start) | copy-done | bytes 1048600
  1.2 0.0 copy-start.1
  1.2 0.7 copy-done.1
  1.9 97.0 %shard_map.46 = bf16[16384,128]{1,0:T(8,128)(2,1)S(1)} custom-call(f32[16384,128]{1,0:T(8,128)} %rhs_ref.1, bf16[16384,512]{1,0:T(8,128)(2,1)} %bitcast.5, f32[32]{0:T(128)S(1)} %bitcast.4, f32[512,512]{1,0:T(8,128)S(1)} %bitcast.3), custom_call_target="tpu_custom_call" | custom-call | flops 2147483648 | bytes 16777216 | tf_op jit(solution)/shard_map/pallas_call | solution.py:334
  98.9 3.7 %convert_element_type.3 = f32[16384,128]{1,0:T(8,128)} convert(bf16[16384,128]{1,0:T(8,128)(2,1)S(1)} %shard_map.46) | non-fusion elementwise | flops 2097152 | bytes 12582912 | tf_op jit(solution)/shard_map/convert_element_type | solution.py:367
Async XLA Ops:
  0.0 1.2 %copy-start = (f32[1,512,512]{2,1,0:T(8,128)S(1)}, f32[1,512,512]{2,1,0:T(8,128)}, u32[]{:S(2)}) copy-start(f32[1,512,512]{2,1,0:T(8,128)} %param.7) | copy-start | bytes 3145732
  1.2 0.7 copy-start.1
